TPU v7x, 32 devices: a whole 2x2x4 slice. The times are simulated.
32 devices in a mesh: groups: 2 (over x), blk: 8 (over z, y), atoms: 2 (over core).
Axes of the slice: x: 2, y: 2, z: 4, core: 2. Of those that a mesh axis runs over, the one named last changes fastest.
Arguments:
- density: bfloat16 [384, 1024], P('groups', 'blk'), parts along dimension 0, may hold values from -6 to 6
- three_centre: bfloat16 [16, 2, 4, 128, 2048], P(('groups', 'blk'), 'atoms'), parts along dimension 0, may hold values from -0.0078125 to 0.0078125
- pattern: int32 [16, 2, 4], P(('groups', 'blk'), 'atoms'), parts along dimension 0, may hold values from 0 to 7, all different within a row
- domain: int32 [16, 2, 2], P(('groups', 'blk')), parts along dimension 0, may hold values from 0 to 1
- owner: int32 [16, 2], P(('groups', 'blk')), parts along dimension 0, may hold values from 0 to 1, each once within a row
- metric: bfloat16 [16, 2, 1024, 1024], P(('groups', 'blk'), 'atoms'), parts along dimension 0, may hold values from -1 to 3, as said below
Outputs:
- exchange: float32 [16, 2, 192, 192], P(('groups', 'blk'), 'atoms'), parts along dimension 0
There are 2 independent parts, one for each index of `groups`. A program takes and returns all parts, laid end to end along the dimension named above; each array names one. Nothing has to cross between parts.
Inputs may be any that keep to these rules, and one draw needn't show every extreme that they name: `pattern`: each device's entries are different tiles. `owner`: each row is an order of the atom groups. `metric`: each matrix is symmetric with a positive diagonal.
All inputs are finite; a program needn't handle non-finite values.
Results may differ from a plain program's by a relative error of at most 0.0013.
Values may be sent and summed in bfloat16 or wider, within the bound.
No kernel may reach another device: no remote copies, remote signals or barrier semaphores. Data moves between devices by JAX's collectives and lax.ppermute only.
A program may use at most 64 MiB of HBM per device.

v0:
```python
import jax
import jax.numpy as jnp
from jax import lax
from jax.sharding import PartitionSpec as P


def partner(block, axis, distance):
    count = lax.axis_size(axis)
    route = []
    for low in range(count):
        high = low | 1 << distance
        if high != low and high < count:
            route += [(low, high), (high, low)]
    return lax.ppermute(block, axis, route)


def fit_term(segment_rows, matrix):
    fitted = jnp.dot(segment_rows, matrix, preferred_element_type=jnp.float32).astype(jnp.bfloat16)
    return lax.dot_general(
        fitted, segment_rows, (((1,), (1,)), ((), ())), preferred_element_type=jnp.float32
    )


def local(density, three_centre, pattern, domain, owner, metric):
    centre = three_centre[0, 0]
    chosen = pattern[0, 0]
    width = centre.shape[1]
    positions = jnp.arange(chosen.shape[0], dtype=jnp.int32)
    initial = jnp.zeros((density.shape[0], centre.shape[2]), jnp.float32)
    piece = lax.all_gather(density, "blk", axis=1, tiled=True)
    tile_count = piece.shape[1] // width

    def add_tile(step, partial_sum):
        tile_piece = lax.dynamic_slice_in_dim(piece, step * width, width, 1)
        matches = chosen == step
        slot_index = jnp.sum(jnp.where(matches, positions, 0))

        def with_tile(current):
            slot_rows = lax.dynamic_index_in_dim(centre, slot_index, 0, keepdims=False)
            return current + jnp.dot(tile_piece, slot_rows, preferred_element_type=jnp.float32)

        def without_tile(current):
            return current

        return lax.cond(jnp.any(matches), with_tile, without_tile, partial_sum)

    halves = lax.fori_loop(0, tile_count, add_tile, initial).astype(jnp.bfloat16)
    own_index = lax.axis_index("atoms")
    segs = domain.shape[2]
    aux = metric.shape[2]
    labels = jnp.arange(domain.shape[1], dtype=jnp.int32)
    targets = jnp.sum(
        jnp.where(domain[0][..., None] == labels, owner[0][None, None, :], 0), axis=-1
    )
    metric_own = metric[0, 0]
    zero_block = jnp.zeros((halves.shape[0], halves.shape[0]), jnp.float32)

    def add_fit(current, segment_rows):
        return current + fit_term(segment_rows, metric_own)

    def keep_sum(current, segment_rows):
        return current

    partner_halves = partner(halves, "atoms", 0)
    result = zero_block
    for source, source_index in ((halves, own_index), (partner_halves, 1 - own_index)):
        source_targets = lax.dynamic_index_in_dim(targets, source_index, 0, keepdims=False)
        for seg_number in range(segs):
            segment_rows = source[:, seg_number * aux : (seg_number + 1) * aux]
            result = lax.cond(
                source_targets[seg_number] == own_index, add_fit, keep_sum, result, segment_rows
            )
    return result[None, None]


def solution(mesh):
    in_specs = (
        P("groups", "blk"),
        P(("groups", "blk"), "atoms", None, None, None),
        P(("groups", "blk"), "atoms", None),
        P(("groups", "blk"), None, None),
        P(("groups", "blk"), None),
        P(("groups", "blk"), "atoms", None, None),
    )
    out_specs = P(("groups", "blk"), "atoms", None, None)
    return jax.shard_map(local, mesh=mesh, in_specs=in_specs, out_specs=out_specs, check_vma=False)
```

profile of v0, /device:TPU:5, one launch (start us, length us, event | category | flops | bytes accessed | tf_op | source)
XLA Modules:
  0.0 76.1 jit_solution(15712342774542263794)
XLA Ops:
  0.0 23.5 %all_gather.3 = bf16[192,1024]{1,0:T(8,128)(2,1)S(1)} all-gather(bf16[192,128]{1,0:T(8,128)(2,1)} %param.18), channel_id=1, replica_groups=mesh['groups'=2,'blk'=8,'atoms'=2] {'blk'}, dimensions={1}, use_global_device_ids=true | all-gather | bytes 442368 | tf_op jit(solution)/shard_map/all_gather | solution.py:30
  23.5 0.2 broadcast_in_dim.42
  23.7 32.5 %while.17 = (s32[]{:T(128)}, f32[192,2048]{1,0:T(8,128)S(1)}, s32[4]{0:T(128)}, bf16[192,1024]{1,0:T(8,128)(2,1)S(1)}, bf16[4,128,2048]{2,1,0:T(8,128)(2,1)}, /*index=5*/s32[]{:T(128)}) while((s32[]{:T(128)}, f32[192,2048]{1,0:T(8,128)S(1)}, s32[4]{0:T(128)}, bf16[192,1024]{1,0:T(8,128)(2,1)S(1)}, bf16[4,128,2048]{2,1,0:T(8,128)(2,1)}, ...), condition=%wide.region_6.7_spmd.clone, body=%wide.region_1.6_spmd.clone.sunk | while | flops 101056536 | bytes 3719459 | solution.py:47
  23.7 1.4 %fusion.31 = (pred[]{:T(512)}, pred[4]{0:T(512)(128)(4,1)S(1)}) fusion(s32[4]{0:T(128)} %get-tuple-element.327, s32[]{:T(128)} %copy.13), kind=kLoop, calls=%fused_computation.28.clone.1 | loop fusion | flops 7 | bytes 25 | tf_op jit(solution)/shard_map/while/body/eval_jaxpr/reduce_or | solution.py:45
  25.7 1.4 %fusion.31 = (pred[]{:T(512)}, pred[4]{0:T(512)(128)(4,1)S(1)}) fusion(s32[4]{0:T(128)} %get-tuple-element.327, s32[]{:T(128)} %copy.13), kind=kLoop, calls=%fused_computation.28.clone.1 | loop fusion | flops 7 | bytes 25 | tf_op jit(solution)/shard_map/while/body/eval_jaxpr/reduce_or | solution.py:45
  27.7 4.1 %conditional.11 = (f32[192,2048]{1,0:T(8,128)S(1)}) conditional(s32[]{:T(128)} %convert_element_type.61, f32[192,2048]{1,0:T(8,128)S(1)} %get-tuple-element.320, (s32[]{:T(128)}, bf16[192,1024]{1,0:T(8,128)(2,1)S(1)}, pred[4]{0:T(512)(128)(4,1)S(1)}, s32[4]{0:T(128)S(1)}, bf16[4,128,2048]{2,1,0:T(8,128)(2,1)}, ...), branch_computations={%region_3.3_spmd, %region_4.5_spmd} | conditional | flops 101056528 | bytes 3719288 | solution.py:45
  27.8 0.7 select_reduce_fusion
  30.3 1.5 %convolution_add_fusion = f32[192,2048]{1,0:T(8,128)S(1)} fusion(f32[192,2048]{1,0:T(8,128)S(1)} %get-tuple-element.216, bf16[4,128,2048]{2,1,0:T(8,128)(2,1)} %get-tuple-element.219, s32[]{:T(128)S(6)} %select_n.34, bf16[192,1024]{1,0:T(8,128)(2,1)S(1)} %get-tuple-element.217, s32[]{:T(128)S(6)} %select_n.32), kind=kOutput, calls=%fused_computation.1 | convolution fusion | flops 101056512 | bytes 3719176 | tf_op jit(solution)/shard_map/while/body/eval_jaxpr/cond/branch_1_fun/dot_general | solution.py:40
  31.8 1.4 %fusion.31 = (pred[]{:T(512)}, pred[4]{0:T(512)(128)(4,1)S(1)}) fusion(s32[4]{0:T(128)} %get-tuple-element.327, s32[]{:T(128)} %copy.13), kind=kLoop, calls=%fused_computation.28.clone.1 | loop fusion | flops 7 | bytes 25 | tf_op jit(solution)/shard_map/while/body/eval_jaxpr/reduce_or | solution.py:45
  33.9 1.4 %fusion.31 = (pred[]{:T(512)}, pred[4]{0:T(512)(128)(4,1)S(1)}) fusion(s32[4]{0:T(128)} %get-tuple-element.327, s32[]{:T(128)} %copy.13), kind=kLoop, calls=%fused_computation.28.clone.1 | loop fusion | flops 7 | bytes 25 | tf_op jit(solution)/shard_map/while/body/eval_jaxpr/reduce_or | solution.py:45
  35.9 1.4 %fusion.31 = (pred[]{:T(512)}, pred[4]{0:T(512)(128)(4,1)S(1)}) fusion(s32[4]{0:T(128)} %get-tuple-element.327, s32[]{:T(128)} %copy.13), kind=kLoop, calls=%fused_computation.28.clone.1 | loop fusion | flops 7 | bytes 25 | tf_op jit(solution)/shard_map/while/body/eval_jaxpr/reduce_or | solution.py:45
  37.9 4.1 %conditional.11 = (f32[192,2048]{1,0:T(8,128)S(1)}) conditional(s32[]{:T(128)} %convert_element_type.61, f32[192,2048]{1,0:T(8,128)S(1)} %get-tuple-element.320, (s32[]{:T(128)}, bf16[192,1024]{1,0:T(8,128)(2,1)S(1)}, pred[4]{0:T(512)(128)(4,1)S(1)}, s32[4]{0:T(128)S(1)}, bf16[4,128,2048]{2,1,0:T(8,128)(2,1)}, ...), branch_computations={%region_3.3_spmd, %region_4.5_spmd} | conditional | flops 101056528 | bytes 3719288 | solution.py:45
  37.9 0.7 select_reduce_fusion
  40.5 1.5 %convolution_add_fusion = f32[192,2048]{1,0:T(8,128)S(1)} fusion(f32[192,2048]{1,0:T(8,128)S(1)} %get-tuple-element.216, bf16[4,128,2048]{2,1,0:T(8,128)(2,1)} %get-tuple-element.219, s32[]{:T(128)S(6)} %select_n.34, bf16[192,1024]{1,0:T(8,128)(2,1)S(1)} %get-tuple-element.217, s32[]{:T(128)S(6)} %select_n.32), kind=kOutput, calls=%fused_computation.1 | convolution fusion | flops 101056512 | bytes 3719176 | tf_op jit(solution)/shard_map/while/body/eval_jaxpr/cond/branch_1_fun/dot_general | solution.py:40
  42.0 1.4 %fusion.31 = (pred[]{:T(512)}, pred[4]{0:T(512)(128)(4,1)S(1)}) fusion(s32[4]{0:T(128)} %get-tuple-element.327, s32[]{:T(128)} %copy.13), kind=kLoop, calls=%fused_computation.28.clone.1 | loop fusion | flops 7 | bytes 25 | tf_op jit(solution)/shard_map/while/body/eval_jaxpr/reduce_or | solution.py:45
  44.0 4.1 %conditional.11 = (f32[192,2048]{1,0:T(8,128)S(1)}) conditional(s32[]{:T(128)} %convert_element_type.61, f32[192,2048]{1,0:T(8,128)S(1)} %get-tuple-element.320, (s32[]{:T(128)}, bf16[192,1024]{1,0:T(8,128)(2,1)S(1)}, pred[4]{0:T(512)(128)(4,1)S(1)}, s32[4]{0:T(128)S(1)}, bf16[4,128,2048]{2,1,0:T(8,128)(2,1)}, ...), branch_computations={%region_3.3_spmd, %region_4.5_spmd} | conditional | flops 101056528 | bytes 3719288 | solution.py:45
  44.0 0.7 select_reduce_fusion
  46.6 1.5 %convolution_add_fusion = f32[192,2048]{1,0:T(8,128)S(1)} fusion(f32[192,2048]{1,0:T(8,128)S(1)} %get-tuple-element.216, bf16[4,128,2048]{2,1,0:T(8,128)(2,1)} %get-tuple-element.219, s32[]{:T(128)S(6)} %select_n.34, bf16[192,1024]{1,0:T(8,128)(2,1)S(1)} %get-tuple-element.217, s32[]{:T(128)S(6)} %select_n.32), kind=kOutput, calls=%fused_computation.1 | convolution fusion | flops 101056512 | bytes 3719176 | tf_op jit(solution)/shard_map/while/body/eval_jaxpr/cond/branch_1_fun/dot_general | solution.py:40
  48.1 1.4 %fusion.31 = (pred[]{:T(512)}, pred[4]{0:T(512)(128)(4,1)S(1)}) fusion(s32[4]{0:T(128)} %get-tuple-element.327, s32[]{:T(128)} %copy.13), kind=kLoop, calls=%fused_computation.28.clone.1 | loop fusion | flops 7 | bytes 25 | tf_op jit(solution)/shard_map/while/body/eval_jaxpr/reduce_or | solution.py:45
  50.1 4.1 %conditional.11 = (f32[192,2048]{1,0:T(8,128)S(1)}) conditional(s32[]{:T(128)} %convert_element_type.61, f32[192,2048]{1,0:T(8,128)S(1)} %get-tuple-element.320, (s32[]{:T(128)}, bf16[192,1024]{1,0:T(8,128)(2,1)S(1)}, pred[4]{0:T(512)(128)(4,1)S(1)}, s32[4]{0:T(128)S(1)}, bf16[4,128,2048]{2,1,0:T(8,128)(2,1)}, ...), branch_computations={%region_3.3_spmd, %region_4.5_spmd} | conditional | flops 101056528 | bytes 3719288 | solution.py:45
  50.1 0.7 select_reduce_fusion
  52.6 1.5 %convolution_add_fusion = f32[192,2048]{1,0:T(8,128)S(1)} fusion(f32[192,2048]{1,0:T(8,128)S(1)} %get-tuple-element.216, bf16[4,128,2048]{2,1,0:T(8,128)(2,1)} %get-tuple-element.219, s32[]{:T(128)S(6)} %select_n.34, bf16[192,1024]{1,0:T(8,128)(2,1)S(1)} %get-tuple-element.217, s32[]{:T(128)S(6)} %select_n.32), kind=kOutput, calls=%fused_computation.1 | convolution fusion | flops 101056512 | bytes 3719176 | tf_op jit(solution)/shard_map/while/body/eval_jaxpr/cond/branch_1_fun/dot_general | solution.py:40
  54.2 1.4 %fusion.31 = (pred[]{:T(512)}, pred[4]{0:T(512)(128)(4,1)S(1)}) fusion(s32[4]{0:T(128)} %get-tuple-element.327, s32[]{:T(128)} %copy.13), kind=kLoop, calls=%fused_computation.28.clone.1 | loop fusion | flops 7 | bytes 25 | tf_op jit(solution)/shard_map/while/body/eval_jaxpr/reduce_or | solution.py:45
  56.2 0.0 copy-start.1
  56.2 0.0 copy-start.2
  56.2 1.0 %convert_element_type.38 = bf16[192,2048]{1,0:T(8,128)(2,1)} convert(f32[192,2048]{1,0:T(8,128)S(1)} %get-tuple-element.241) | non-fusion elementwise | flops 393216 | bytes 2359296 | tf_op jit(solution)/shard_map/convert_element_type | solution.py:47
  57.2 4.7 %collective-permute-start = (bf16[192,2048]{1,0:T(8,128)(2,1)}, bf16[192,2048]{1,0:T(8,128)(2,1)S(1)}, u32[]{:S(2)}, u32[]{:S(2)}) collective-permute-start(bf16[192,2048]{1,0:T(8,128)(2,1)} %convert_element_type.38), channel_id=1, source_target_pairs={{0,1},{1,0},{2,3},{3,2},{4,5},{5,4},{6,7},{7,6},{8,9},{9,8},{10,11... | collective-permute-start | bytes 2359304 | tf_op jit(solution)/shard_map/ppermute | solution.py:14
  61.8 0.0 copy-done.1
  61.8 0.0 copy-done.2
  61.8 0.2 fusion.22
  62.1 0.7 fusion.24
  65.3 2.6 %conditional.5 = (f32[192,192]{1,0:T(8,128)S(1)}) conditional(s32[]{:T(128)} %convert_element_type.37, () %tuple.68, (bf16[192,2048]{1,0:T(8,128)(2,1)}, bf16[1024,1024]{1,0:T(8,128)(2,1)}) %tuple.115), branch_computations={%region_7.8_spmd, %region_8.9_spmd} | conditional | flops 478347264 | bytes 3031048 | solution.py:70
  65.3 2.6 %fusion.6 = f32[192,192]{1,0:T(8,128)S(1)} fusion(bf16[1024,1024]{1,0:T(8,128)(2,1)} %get-tuple-element.230, bf16[192,2048]{1,0:T(8,128)(2,1)} %get-tuple-element.242), kind=kOutput, calls=%fused_computation.8 | convolution fusion | flops 478347264 | bytes 3031040 | tf_op jit(solution)/shard_map/cond/branch_1_fun/dot_general | solution.py:19
  67.9 2.6 %conditional.6 = (f32[192,192]{1,0:T(8,128)S(1)}) conditional(s32[]{:T(128)} %convert_element_type.36, f32[192,192]{1,0:T(8,128)S(1)} %get-tuple-element.336, (bf16[192,2048]{1,0:T(8,128)(2,1)}, bf16[1024,1024]{1,0:T(8,128)(2,1)}, f32[192,192]{1,0:T(8,128)S(1)}) %tuple.116), branch_computations={%region_9.10_spmd, %region_10.11_spmd} | conditional | flops 478384128 | bytes 3178504 | solution.py:70
  67.9 2.6 %fusion.10 = f32[192,192]{1,0:T(8,128)S(1)} fusion(f32[192,192]{1,0:T(8,128)S(1)} %get-tuple-element.231, bf16[1024,1024]{1,0:T(8,128)(2,1)} %get-tuple-element.233, bf16[192,2048]{1,0:T(8,128)(2,1)} %get-tuple-element.243), kind=kOutput, calls=%fused_computation.12 | convolution fusion | flops 478384128 | bytes 3178496 | tf_op jit(solution)/shard_map/cond/branch_1_fun/dot_general | solution.py:19
  70.5 0.0 collective-permute-done
  70.5 2.4 %conditional.7 = (f32[192,192]{1,0:T(8,128)S(1)}) conditional(s32[]{:T(128)} %convert_element_type.35, f32[192,192]{1,0:T(8,128)S(1)} %get-tuple-element.337, (bf16[192,2048]{1,0:T(8,128)(2,1)S(1)}, bf16[1024,1024]{1,0:T(8,128)(2,1)}, f32[192,192]{1,0:T(8,128)S(1)}) %tuple.117), branch_computations={%region_11.12_spmd, %region_12.13_spmd} | conditional | flops 478384128 | bytes 3178504 | solution.py:70
  70.5 2.4 %fusion.14 = f32[192,192]{1,0:T(8,128)S(1)} fusion(f32[192,192]{1,0:T(8,128)S(1)} %get-tuple-element.234, bf16[1024,1024]{1,0:T(8,128)(2,1)} %get-tuple-element.236, bf16[192,2048]{1,0:T(8,128)(2,1)S(1)} %get-tuple-element.244), kind=kOutput, calls=%fused_computation.16 | convolution fusion | flops 478384128 | bytes 3178496 | tf_op jit(solution)/shard_map/cond/branch_1_fun/dot_general | solution.py:19
  72.9 2.4 %conditional.8 = (f32[1,1,192,192]{3,2,1,0:T(8,128)S(1)}) conditional(s32[]{:T(128)} %convert_element_type.34, f32[192,192]{1,0:T(8,128)S(1)} %get-tuple-element.338, (bf16[192,2048]{1,0:T(8,128)(2,1)S(1)}, bf16[1024,1024]{1,0:T(8,128)(2,1)}, f32[192,192]{1,0:T(8,128)S(1)}) %tuple.118), branch_computations={%region_13.14_spmd, %region_14.15_spmd} | conditional | flops 478384128 | bytes 3178504 | solution.py:70
  73.0 2.4 %fusion.19 = f32[1,1,192,192]{3,2,1,0:T(8,128)S(1)} fusion(f32[192,192]{1,0:T(8,128)S(1)} %get-tuple-element.237, bf16[1024,1024]{1,0:T(8,128)(2,1)} %get-tuple-element.239, bf16[192,2048]{1,0:T(8,128)(2,1)S(1)} %get-tuple-element.238), kind=kOutput, calls=%fused_computation.21 | convolution fusion | flops 478384128 | bytes 3178496 | tf_op jit(solution)/shard_map/cond/branch_1_fun/dot_general | solution.py:19
  75.4 0.0 copy-start
  75.4 0.7 copy-done
  (13 shorter events, 0.1 us)
Async XLA Ops:
  56.2 5.7 %copy-start.1 = (s32[1,2,2]{2,1,0:T(2,128)S(1)}, s32[1,2,2]{2,1,0:T(2,128)}, u32[]{:S(2)}) copy-start(s32[1,2,2]{2,1,0:T(2,128)} %param.21) | copy-start | bytes 52
  56.2 5.7 %copy-start.2 = (s32[1,2]{1,0:T(1,128)S(1)}, s32[1,2]{1,0:T(1,128)}, u32[]{:S(2)}) copy-start(s32[1,2]{1,0:T(1,128)} %param.22) | copy-start | bytes 28
  57.2 13.3 %collective-permute-start = (bf16[192,2048]{1,0:T(8,128)(2,1)}, bf16[192,2048]{1,0:T(8,128)(2,1)S(1)}, u32[]{:S(2)}, u32[]{:S(2)}) collective-permute-start(bf16[192,2048]{1,0:T(8,128)(2,1)} %convert_element_type.38), channel_id=1, source_target_pairs={{0,1},{1,0},{2,3},{3,2},{4,5},{5,4},{6,7},{7,6},{8,9},{9,8},{10,11... | collective-permute-start | bytes 2359304 | tf_op jit(solution)/shard_map/ppermute | solution.py:14
  75.4 0.7 copy-start
where the time goes:
time: 76 us; the launch traced here: 76.1 us
  blocking collectives  23.5 us (31%)
  matrix products  15.9 us (21%)
  other arithmetic  14.9 us (20%)
  loops' own time  13 us (17%)
  starting transfers between devices  4.66 us (6%)
  between operations  2.68 us (4%)
  local copies, waits for them, and re-layouts  1.53 us (2%)
    all_gather x1, blocking collectives, local(): piece = lax.all_gather(density, 'blk', axis=1, tiled=True)  23.5 us
    reduce_or x8, other arithmetic, add_tile(): return lax.cond(jnp.any(matches), with_tile, without_tile, partial_sum)  10.9 us
    dot_general x4, matrix products, fit_term(): lax.dot_general(fitted, segment_rows, (((1,), (1,)), ((), ())), preferred...  9.97 us
    another operation x8, loops' own time, add_tile(): return lax.cond(jnp.any(matches), with_tile, without_tile, partial_sum)  7.63 us
    dot_general x4, matrix products, with_tile(): jnp.dot(tile_piece, slot_rows, preferred_element_type=jnp.float32)  5.9 us
    another operation x1, loops' own time, local(): lax.fori_loop(0, tile_count, add_tile, initial).astype(jnp.bfloat16)  5.26 us
    ppermute x1, starting transfers between devices, partner(): return lax.ppermute(block, axis, route)  4.66 us
    reduce_sum x4, other arithmetic, add_tile(): slot_index = jnp.sum(jnp.where(matches, positions, 0))  2.79 us
  transfers between devices with their start and end apart: 1, of which 0 were waited for; matrix products, arithmetic and copies ran while one was open for 8% of the time, Pallas kernels for 0%

commit v1 on v0

v1 whole, which is shorter than its diff:
```python
import functools
import jax
import jax.numpy as jnp
from jax import lax
from jax.experimental import pallas as pl
from jax.experimental.pallas import tpu as pltpu
from jax.sharding import PartitionSpec as P

AXES = ("blk", "atoms")


def between_blocks(block, count, even, odd):
    pairs = []
    for b in range(count):
        pairs.append((2 * b, 2 * (b ^ even)))
        pairs.append((2 * b + 1, 2 * (b ^ odd) + 1))
    return lax.ppermute(block, AXES, pairs)


def swap_cores(block):
    return lax.ppermute(block, "atoms", [(0, 1), (1, 0)])


def far(array):
    return pltpu.with_memory_space_constraint(array, pltpu.HBM)


def routes(count):
    return [(k, k - 1) for k in range(count - 1, 2, -2)] + [(1, 1)]


def exchange_kernel(plan, count, *refs):
    indices_hbm = refs[:4]
    tiles = refs[4 : 4 + count]
    centre, centre_other, metric, out = refs[4 + count : 8 + count]
    table, dens, rows, matrix, sem = refs[8 + count : 13 + count]
    indices = refs[13 + count : 17 + count]
    index_sem = refs[17 + count]
    pattern, pattern_other, domain, owner = indices
    block = lax.axis_index("blk")
    core = lax.axis_index("atoms")
    segs = domain.shape[2]
    slots, width = centre.shape[2], centre.shape[3]
    aux = metric.shape[2]

    def load(source, seg):
        hbm = centre if source == 0 else centre_other
        return pltpu.make_async_copy(
            hbm.at[0, 0, :, :, pl.ds(seg * aux, aux)], rows.at[source, seg], sem.at[source * segs + seg]
        )

    index_loads = [
        pltpu.make_async_copy(far, near, index_sem.at[i]) for i, (far, near) in enumerate(zip(indices_hbm, indices))
    ]
    own_tile = pltpu.make_async_copy(tiles[0], table.at[block], index_sem.at[4])
    for copy in index_loads + [own_tile]:
        copy.start()
    for seg in range(segs):
        load(0, seg).start()
    load_metric = pltpu.make_async_copy(metric.at[0, 0], matrix, sem.at[2 * segs])
    load_metric.start()
    for seg in range(segs):
        load(1, seg).start()

    position = 1
    for even, odd in plan:
        if even == odd:
            table[block ^ even] = tiles[position][...]
            position += 1
        else:
            table[block ^ jnp.where(core == 0, even, odd)] = tiles[position][...]
            table[block ^ jnp.where(core == 0, odd, even)] = tiles[position + 1][...]
            position += 2
    for copy in index_loads + [own_tile]:
        copy.wait()
    for source, chosen in enumerate((pattern, pattern_other)):
        for slot in range(slots):
            dens[source, :, slot * width : (slot + 1) * width] = table[chosen[0, 0, slot]]

    out[...] = jnp.zeros_like(out)
    waited = []
    for source in range(2):
        origin = core if source == 0 else 1 - core
        for seg in range(segs):
            load(source, seg).wait()
            if not waited:
                load_metric.wait()
                waited.append(True)

            @pl.when(owner[0, domain[0, origin, seg]] == core)
            def _():
                wide = rows[source, seg].reshape(slots * width, aux)
                half = jnp.dot(dens[source], wide, preferred_element_type=jnp.float32).astype(jnp.bfloat16)
                fitted = jnp.dot(half, matrix[...], preferred_element_type=jnp.float32).astype(jnp.bfloat16)
                out[0, 0] += lax.dot_general(
                    fitted, half, (((1,), (1,)), ((), ())), preferred_element_type=jnp.float32
                )


def local(count, density, three_centre, pattern, domain, owner, metric):
    nocc = density.shape[0]
    slots, width = three_centre.shape[2:4]
    segs, aux = domain.shape[2], metric.shape[2]
    plan = routes(count)
    received = [between_blocks(density, count, even, odd) for even, odd in plan]
    pattern_other = swap_cores(pattern)
    centre_other = swap_cores(three_centre)
    tiles = [density]
    for (even, odd), tile in zip(plan, received):
        tiles.append(tile)
        if even != odd:
            tiles.append(swap_cores(tile))
    vmem = pl.BlockSpec(memory_space=pltpu.VMEM)
    hbm = pl.BlockSpec(memory_space=pltpu.HBM)
    return pl.pallas_call(
        functools.partial(exchange_kernel, plan, count),
        out_shape=jax.ShapeDtypeStruct((1, 1, nocc, nocc), jnp.float32),
        in_specs=[hbm] * 5 + [vmem] * (count - 1) + [hbm] * 3,
        out_specs=vmem,
        scratch_shapes=[
            pltpu.VMEM((count, nocc, width), jnp.bfloat16),
            pltpu.VMEM((2, nocc, slots * width), jnp.bfloat16),
            pltpu.VMEM((2, segs, slots, width, aux), jnp.bfloat16),
            pltpu.VMEM((aux, aux), jnp.bfloat16),
            pltpu.SemaphoreType.DMA((2 * segs + 1,)),
            pltpu.SMEM(pattern.shape, jnp.int32),
            pltpu.SMEM(pattern.shape, jnp.int32),
            pltpu.SMEM(domain.shape, jnp.int32),
            pltpu.SMEM(owner.shape, jnp.int32),
            pltpu.SemaphoreType.DMA((5,)),
        ],
        compiler_params=pltpu.CompilerParams(vmem_limit_bytes=40 * 1024 * 1024),
    )(
        far(pattern), pattern_other, far(domain), far(owner), far(density), *tiles[1:],
        far(three_centre), centre_other, far(metric),
    )


def solution(mesh):
    in_specs = (
        P("groups", "blk"),
        P(("groups", "blk"), "atoms", None, None, None),
        P(("groups", "blk"), "atoms", None),
        P(("groups", "blk"), None, None),
        P(("groups", "blk"), None),
        P(("groups", "blk"), "atoms", None, None),
    )
    out_specs = P(("groups", "blk"), "atoms", None, None)
    body = functools.partial(local, mesh.shape["blk"])
    return jax.shard_map(body, mesh=mesh, in_specs=in_specs, out_specs=out_specs, check_vma=False)
```

time: 76 us -> 20.4 us (0.27)
  the two profiles are of different devices: /device:TPU:5 before, /device:TPU:1 now
where the time goes in v1:
time: 20.4 us; the launch traced here: 20.6 us
  starting transfers between devices  12.7 us (62%)
  Pallas kernels  6.02 us (30%)
  waiting for transfers between devices  1.84 us (9%)
    ppermute x5, starting transfers between devices, swap_cores(): return lax.ppermute(block, 'atoms', [(0, 1), (1, 0)])  7.59 us
    pallas_call x1, Pallas kernels, local(): pl.pallas_call(functools.partial(exchange_kernel, plan, count), out_shape...  6.02 us
    ppermute x4, starting transfers between devices, between_blocks(): return lax.ppermute(block, AXES, pairs)  5.12 us
    ppermute x5, waiting for transfers between devices, swap_cores(): return lax.ppermute(block, 'atoms', [(0, 1), (1, 0)])  1.83 us
  transfers between devices with their start and end apart: 9, of which 2 were waited for; matrix products, arithmetic and copies ran while one was open for 0% of the time, Pallas kernels for 0%

profile of v1, /device:TPU:1, one launch (start us, length us, event | category | flops | bytes accessed | tf_op | source)
XLA Modules:
  0.0 20.6 jit_solution(10927296207775546061)
XLA Ops:
  0.0 0.1 collective-permute-start.8
  0.1 2.7 %collective-permute-start.5 = (bf16[192,128]{1,0:T(8,128)(2,1)}, bf16[192,128]{1,0:T(8,128)(2,1)S(1)}, u32[]{:S(2)}, u32[]{:S(2)}) collective-permute-start(bf16[192,128]{1,0:T(8,128)(2,1)} %refs_4_.1), channel_id=1, source_target_pairs={{0,6},{1,5},{2,4},{3,7},{4,2},{5,1},{6,0},{7,3},{8,14},{9,13},{10,... | collective-permute-start | bytes 147464 | tf_op jit(solution)/shard_map/ppermute | solution.py:17
  2.8 2.3 %collective-permute-start.3 = (bf16[192,128]{1,0:T(8,128)(2,1)}, bf16[192,128]{1,0:T(8,128)(2,1)S(1)}, u32[]{:S(2)}, u32[]{:S(2)}) collective-permute-start(bf16[192,128]{1,0:T(8,128)(2,1)} %refs_4_.1), channel_id=1, source_target_pairs={{0,10},{1,9},{2,8},{3,11},{4,14},{5,13},{6,12},{7,15},{8,2},{9,1},... | collective-permute-start | bytes 147464 | tf_op jit(solution)/shard_map/ppermute | solution.py:17
  5.1 0.0 collective-permute-start.1
  5.1 2.6 %collective-permute-start = (s32[1,1,4]{2,1,0:T(1,128)}, s32[1,1,4]{2,1,0:T(1,128)S(1)}, u32[]{:S(2)}, u32[]{:S(2)}) collective-permute-start(s32[1,1,4]{2,1,0:T(1,128)} %refs_0_.1), channel_id=1, source_target_pairs={{0,1},{1,0},{2,3},{3,2},{4,5},{5,4},{6,7},{7,6},{8,9},{9,8},{10,11... | collective-permute-start | bytes 56 | tf_op jit(solution)/shard_map/ppermute | solution.py:21
  7.8 1.0 %collective-permute-done.refs_1_ = s32[1,1,4]{2,1,0:T(1,128)S(1)} collective-permute-done((s32[1,1,4]{2,1,0:T(1,128)}, s32[1,1,4]{2,1,0:T(1,128)S(1)}, u32[]{:S(2)}, u32[]{:S(2)}) %collective-permute-start) | collective-permute-done | bytes 48 | tf_op jit(solution)/shard_map/ppermute | solution.py:21
  8.7 0.1 collective-permute-start.7
  8.8 0.0 collective-permute-done.5.refs_9_
  8.8 0.6 %collective-permute-start.6 = (bf16[192,128]{1,0:T(8,128)(2,1)S(1)}, bf16[192,128]{1,0:T(8,128)(2,1)S(1)}, u32[]{:S(2)}, u32[]{:S(2)}) collective-permute-start(bf16[192,128]{1,0:T(8,128)(2,1)S(1)} %collective-permute-done.5.refs_9_), channel_id=1, source_target_pairs={{0,1},{1,0},{2,3},{3,2},{4,5},{5,4},{6,7},{7,6},{8,9},{9,8},{10,11... | collective-permute-start | bytes 147464 | tf_op jit(solution)/shard_map/ppermute | solution.py:21
  9.4 0.0 collective-permute-done.3.refs_7_
  9.4 1.6 %collective-permute-start.4 = (bf16[192,128]{1,0:T(8,128)(2,1)S(1)}, bf16[192,128]{1,0:T(8,128)(2,1)S(1)}, u32[]{:S(2)}, u32[]{:S(2)}) collective-permute-start(bf16[192,128]{1,0:T(8,128)(2,1)S(1)} %collective-permute-done.3.refs_7_), channel_id=1, source_target_pairs={{0,1},{1,0},{2,3},{3,2},{4,5},{5,4},{6,7},{7,6},{8,9},{9,8},{10,11... | collective-permute-start | bytes 147464 | tf_op jit(solution)/shard_map/ppermute | solution.py:21
  11.0 0.0 collective-permute-done.1.refs_5_
  11.0 2.7 %collective-permute-start.2 = (bf16[192,128]{1,0:T(8,128)(2,1)S(1)}, bf16[192,128]{1,0:T(8,128)(2,1)S(1)}, u32[]{:S(2)}, u32[]{:S(2)}) collective-permute-start(bf16[192,128]{1,0:T(8,128)(2,1)S(1)} %collective-permute-done.1.refs_5_), channel_id=1, source_target_pairs={{0,1},{1,0},{2,3},{3,2},{4,5},{5,4},{6,7},{7,6},{8,9},{9,8},{10,11... | collective-permute-start | bytes 147464 | tf_op jit(solution)/shard_map/ppermute | solution.py:21
  13.7 0.0 collective-permute-done.7.refs_11_
  13.7 0.0 collective-permute-done.6.refs_10_
  13.7 0.0 collective-permute-done.4.refs_8_
  13.7 0.9 %collective-permute-done.2.refs_6_ = bf16[192,128]{1,0:T(8,128)(2,1)S(1)} collective-permute-done((bf16[192,128]{1,0:T(8,128)(2,1)S(1)}, bf16[192,128]{1,0:T(8,128)(2,1)S(1)}, u32[]{:S(2)}, u32[]{:S(2)}) %collective-permute-start.2) | collective-permute-done | bytes 49184 | tf_op jit(solution)/shard_map/ppermute | solution.py:21
  14.6 0.0 collective-permute-done.8.refs_13_
  14.6 6.0 %shard_map.64 = f32[1,1,192,192]{3,2,1,0:T(8,128)} custom-call(s32[1,1,4]{2,1,0:T(1,128)} %refs_0_.1, s32[1,1,4]{2,1,0:T(1,128)S(1)} %collective-permute-done.refs_1_, s32[1,2,2]{2,1,0:T(2,128)} %refs_2_.1, s32[1,2]{1,0:T(1,128)} %refs_3_.1, bf16[192,128]{1,0:T(8,128)(2,1)} %refs_4_.1, bf16[192,128]{1,0:T(8,128)(2,1)S(1)} %collective-permute-done.1.refs_5_, ...), custom_call_target="tpu_custom_call" | custom-call | tf_op jit(solution)/shard_map/pallas_call | solution.py:115
Async XLA Ops:
  0.0 14.6 %collective-permute-start.8 = (bf16[1,1,4,128,2048]{4,3,2,1,0:T(8,128)(2,1)}, bf16[1,1,4,128,2048]{4,3,2,1,0:T(8,128)(2,1)S(1)}, u32[]{:S(2)}, u32[]{:S(2)}) collective-permute-start(bf16[1,1,4,128,2048]{4,3,2,1,0:T(8,128)(2,1)} %refs_12_.1), channel_id=1, source_target_pairs={{0,1},{1,0},{2,3},{3,2},{4,5},{5,4},{6,7},{7,6},{8,9},{9,8},{10,11... | collective-permute-start | bytes 6291464 | tf_op jit(solution)/shard_map/ppermute | solution.py:21
  0.1 8.7 %collective-permute-start.5 = (bf16[192,128]{1,0:T(8,128)(2,1)}, bf16[192,128]{1,0:T(8,128)(2,1)S(1)}, u32[]{:S(2)}, u32[]{:S(2)}) collective-permute-start(bf16[192,128]{1,0:T(8,128)(2,1)} %refs_4_.1), channel_id=1, source_target_pairs={{0,6},{1,5},{2,4},{3,7},{4,2},{5,1},{6,0},{7,3},{8,14},{9,13},{10,... | collective-permute-start | bytes 147464 | tf_op jit(solution)/shard_map/ppermute | solution.py:17
  2.8 6.6 %collective-permute-start.3 = (bf16[192,128]{1,0:T(8,128)(2,1)}, bf16[192,128]{1,0:T(8,128)(2,1)S(1)}, u32[]{:S(2)}, u32[]{:S(2)}) collective-permute-start(bf16[192,128]{1,0:T(8,128)(2,1)} %refs_4_.1), channel_id=1, source_target_pairs={{0,10},{1,9},{2,8},{3,11},{4,14},{5,13},{6,12},{7,15},{8,2},{9,1},... | collective-permute-start | bytes 147464 | tf_op jit(solution)/shard_map/ppermute | solution.py:17
  5.1 5.9 %collective-permute-start.1 = (bf16[192,128]{1,0:T(8,128)(2,1)}, bf16[192,128]{1,0:T(8,128)(2,1)S(1)}, u32[]{:S(2)}, u32[]{:S(2)}) collective-permute-start(bf16[192,128]{1,0:T(8,128)(2,1)} %refs_4_.1), channel_id=1, source_target_pairs={{0,14},{1,13},{2,12},{3,15},{4,10},{5,9},{6,8},{7,11},{8,6},{9,5},... | collective-permute-start | bytes 147464 | tf_op jit(solution)/shard_map/ppermute | solution.py:17
  5.1 3.6 %collective-permute-start = (s32[1,1,4]{2,1,0:T(1,128)}, s32[1,1,4]{2,1,0:T(1,128)S(1)}, u32[]{:S(2)}, u32[]{:S(2)}) collective-permute-start(s32[1,1,4]{2,1,0:T(1,128)} %refs_0_.1), channel_id=1, source_target_pairs={{0,1},{1,0},{2,3},{3,2},{4,5},{5,4},{6,7},{7,6},{8,9},{9,8},{10,11... | collective-permute-start | bytes 56 | tf_op jit(solution)/shard_map/ppermute | solution.py:21
  8.7 5.0 %collective-permute-start.7 = (bf16[192,128]{1,0:T(8,128)(2,1)}, bf16[192,128]{1,0:T(8,128)(2,1)S(1)}, u32[]{:S(2)}, u32[]{:S(2)}) collective-permute-start(bf16[192,128]{1,0:T(8,128)(2,1)} %refs_4_.1), channel_id=1, source_target_pairs={{0,2},{1,3},{2,0},{3,1},{4,6},{5,7},{6,4},{7,5},{8,10},{9,11},{10,... | collective-permute-start | bytes 147464 | tf_op jit(solution)/shard_map/ppermute | solution.py:17
  8.8 4.9 %collective-permute-start.6 = (bf16[192,128]{1,0:T(8,128)(2,1)S(1)}, bf16[192,128]{1,0:T(8,128)(2,1)S(1)}, u32[]{:S(2)}, u32[]{:S(2)}) collective-permute-start(bf16[192,128]{1,0:T(8,128)(2,1)S(1)} %collective-permute-done.5.refs_9_), channel_id=1, source_target_pairs={{0,1},{1,0},{2,3},{3,2},{4,5},{5,4},{6,7},{7,6},{8,9},{9,8},{10,11... | collective-permute-start | bytes 147464 | tf_op jit(solution)/shard_map/ppermute | solution.py:21
  9.4 4.3 %collective-permute-start.4 = (bf16[192,128]{1,0:T(8,128)(2,1)S(1)}, bf16[192,128]{1,0:T(8,128)(2,1)S(1)}, u32[]{:S(2)}, u32[]{:S(2)}) collective-permute-start(bf16[192,128]{1,0:T(8,128)(2,1)S(1)} %collective-permute-done.3.refs_7_), channel_id=1, source_target_pairs={{0,1},{1,0},{2,3},{3,2},{4,5},{5,4},{6,7},{7,6},{8,9},{9,8},{10,11... | collective-permute-start | bytes 147464 | tf_op jit(solution)/shard_map/ppermute | solution.py:21
  11.0 3.6 %collective-permute-start.2 = (bf16[192,128]{1,0:T(8,128)(2,1)S(1)}, bf16[192,128]{1,0:T(8,128)(2,1)S(1)}, u32[]{:S(2)}, u32[]{:S(2)}) collective-permute-start(bf16[192,128]{1,0:T(8,128)(2,1)S(1)} %collective-permute-done.1.refs_5_), channel_id=1, source_target_pairs={{0,1},{1,0},{2,3},{3,2},{4,5},{5,4},{6,7},{7,6},{8,9},{9,8},{10,11... | collective-permute-start | bytes 147464 | tf_op jit(solution)/shard_map/ppermute | solution.py:21
